TPU v7x, 32 devices: a whole 2x2x4 slice. The times are simulated.
32 devices in a mesh: row: 8 (over y, x, core), col: 4 (over z).
Axes of the slice: x: 2, y: 2, z: 4, core: 2. Of those that a mesh axis runs over, the one named last changes fastest.
Arguments:
- trailing_in: float32 [2, 8, 256, 4, 4, 256], P(None, 'row', None, None, 'col'), may hold values from 0 to 4, as said below
Outputs:
- factored: float32 [2, 8, 256, 4, 4, 256], P(None, 'row', None, None, 'col')
Inputs may be any that keep to these rules, and one draw needn't show every extreme that they name: `trailing_in`: the matrix is symmetric and positive definite.
All inputs are finite; a program needn't handle non-finite values.
Results may differ from a plain program's by a relative error of at most 0.0003.
Values sent between devices are 32-bit elements; how exact they have to be, the bound alone decides.
No kernel may reach another device: no remote copies, remote signals or barrier semaphores. Data moves between devices by JAX's collectives and lax.ppermute only.
A program may use at most 64 MiB of HBM per device.

v0:
```python
import functools

import jax
import jax.numpy as jnp
from jax import lax
from jax.experimental import pallas as pl
from jax.experimental.pallas import tpu as pltpu
from jax.sharding import PartitionSpec as P

NB = 256
HALF = 128
SUB = 8
HIGHEST = lax.Precision.HIGHEST
HIGH = lax.Precision.HIGH


def mm(a, b, precision=HIGHEST):
    return lax.dot_general(
        a, b, (((1,), (0,)), ((), ())), precision=precision, preferred_element_type=jnp.float32
    )


def mm_t(a, b, precision=HIGHEST):
    return lax.dot_general(
        a, b, (((1,), (1,)), ((), ())), precision=precision, preferred_element_type=jnp.float32
    )


def t_mm(a, b, precision=HIGHEST):
    return lax.dot_general(
        a, b, (((0,), (0,)), ((), ())), precision=precision, preferred_element_type=jnp.float32
    )


def spread(x):
    return jnp.broadcast_to(x, (SUB, HALF))


def factor_half(s):
    groups = HALF // SUB
    lane = lax.broadcasted_iota(jnp.int32, (SUB, HALF), 1)
    sub = lax.broadcasted_iota(jnp.int32, (SUB, HALF), 0)
    rows = [s[SUB * g : SUB * (g + 1), :] for g in range(groups)]
    own_diagonal = [jnp.where(lane == sub + SUB * g, rows[g], 0.0) for g in range(groups)]
    diagonal = spread(jnp.sum(sum(own_diagonal), axis=0, keepdims=True))
    scale = lax.rsqrt(diagonal)
    unscale = diagonal * scale
    eyes = []
    for g in range(groups):
        down = spread(lax.rsqrt(jnp.sum(own_diagonal[g], axis=1, keepdims=True)))
        rows[g] = (rows[g] * scale) * down
        eyes.append(jnp.where(lane == sub + SUB * g, 1.0, 0.0).astype(jnp.float32))
    out_u, out_x = [], []
    for g in range(groups):
        base = SUB * g
        own = rows[g]
        own_x = eyes[g]
        a = {}
        for j in range(SUB):
            column = spread(own[:, base + j : base + j + 1])
            for i in range(j + 1):
                a[i, j] = spread(column[i : i + 1, :])
        near = None
        if g + 1 < groups:
            near = [spread(rows[g + 1][:, base + j : base + j + 1]) for j in range(SUB)]
        u = [spread(own[i : i + 1, :]) for i in range(SUB)]
        x = [spread(own_x[i : i + 1, :]) for i in range(SUB)]
        r = [None] * SUB
        l = {}
        for k in range(0, SUB, 2):
            p, q, t = a[k, k], a[k, k + 1], a[k + 1, k + 1]
            r[k] = lax.rsqrt(p)
            root = lax.rsqrt(p * t - q * q)
            both = r[k] * root
            r[k + 1] = (p * r[k]) * root
            l[k, k + 1] = q * r[k]
            for j in range(k + 2, SUB):
                l[k, j] = a[k, j] * r[k]
                l[k + 1, j] = (p * a[k + 1, j] - q * a[k, j]) * both
            for i in range(k + 2, SUB):
                for j in range(i, SUB):
                    a[i, j] = (a[i, j] - l[k, i] * l[k, j]) - l[k + 1, i] * l[k + 1, j]
            for m in (k, k + 1):
                u[m] = u[m] * r[m]
                x[m] = x[m] * r[m]
                if near is not None:
                    near[m] = near[m] * r[m]
                for i in range(m + 1, SUB):
                    u[i] = u[i] - l[m, i] * u[m]
                    x[i] = x[i] - l[m, i] * x[m]
                    if near is not None:
                        near[i] = near[i] - l[m, i] * near[m]
        final_u, final_x = u[0], x[0]
        for i in range(1, SUB):
            final_u = jnp.where(sub == i, u[i], final_u)
            final_x = jnp.where(sub == i, x[i], final_x)
        out_u.append(jnp.where(lane >= sub + base, final_u * unscale, 0.0))
        out_x.append(final_x * scale)
        if near is not None:
            nxt, nxt_x = rows[g + 1], eyes[g + 1]
            for k in range(SUB):
                nxt = nxt - near[k] * u[k]
                nxt_x = nxt_x - near[k] * x[k]
        if g + 2 < groups:
            v, vx = list(u), list(x)
            for i in reversed(range(SUB)):
                for j in range(i + 1, SUB):
                    v[i] = v[i] - l[i, j] * v[j]
                    vx[i] = vx[i] - l[i, j] * vx[j]
                v[i] = v[i] * r[i]
                vx[i] = vx[i] * r[i]
            for h in range(g + 2, groups):
                far, far_x = rows[h], eyes[h]
                for j in range(SUB):
                    c = spread(rows[h][:, base + j : base + j + 1])
                    far = far - c * v[j]
                    far_x = far_x - c * vx[j]
                rows[h], eyes[h] = far, far_x
        if near is not None:
            rows[g + 1], eyes[g + 1] = nxt, nxt_x
    return jnp.concatenate(out_u, axis=0), jnp.concatenate(out_x, axis=0)


def finish_blocks(u11, u12, x11, rest, u_ref, x_ref):
    zero = jnp.zeros((HALF, HALF), jnp.float32)
    u22, x22 = factor_half(rest)
    u_ref[:HALF, :HALF] = u11
    u_ref[:HALF, HALF:] = u12
    u_ref[HALF:, :HALF] = zero
    u_ref[HALF:, HALF:] = u22
    x_ref[:HALF, :HALF] = x11
    x_ref[:HALF, HALF:] = zero
    x_ref[HALF:, :HALF] = -mm(x22, t_mm(u12, x11))
    x_ref[HALF:, HALF:] = x22


def factor_blocks(s11, s12, s22, u_ref, x_ref):
    u11, x11 = factor_half(s11)
    u12 = mm(x11, s12)
    finish_blocks(u11, u12, x11, s22 - t_mm(u12, u12), u_ref, x_ref)


def tile_from(ref, start, stride):
    return jnp.concatenate(
        [ref[pl.ds(start, NB, stride=stride), :], ref[pl.ds(start + 1, NB, stride=stride), :]], axis=1
    )


def pack_kernel(loc_rows, loc_cols, own, top_a, top_b, *left):
    stride = 2 * loc_cols
    for a in range(loc_rows):
        left[a][...] = tile_from(own, a * NB * stride, stride)
    half = HALF * stride
    top_a[...] = own[:half, :]
    top_b[...] = own[half : 2 * half, :]


def start_blocks(s, u_ref, x_ref, rest_ref):
    u11, x11 = factor_half(s[:HALF, :HALF])
    u12 = mm(x11, s[:HALF, HALF:])
    u_ref[:HALF, :] = u11
    u_ref[HALF:, :] = u12
    x_ref[...] = x11
    rest_ref[...] = s[HALF:, HALF:] - t_mm(u12, u12)


def first_kernel(pos, mine, other, u_ref, x_ref):
    s = jnp.where(pos[0] % 2 == 0, mine[...], other[...])
    factor_blocks(s[:HALF, :HALF], s[:HALF, HALF:], s[HALF:, HALF:], u_ref, x_ref)


def second_kernel(pos, x0, mine0, mine1, other0, other1, u01_ref, u_ref, x_ref, rest_ref):
    even = pos[0] % 2 == 0
    u01 = mm(x0[...], jnp.where(even, mine1[...], other1[...]))
    u01_ref[...] = u01
    start_blocks(jnp.where(even, other0[...], mine1[...]) - t_mm(u01, u01), u_ref, x_ref, rest_ref)


def third_kernel(x0, u01, ua, xa, rest, u_ref, x_ref, w_ref):
    finish_blocks(ua[:HALF, :], ua[HALF:, :], xa[...], rest[...], u_ref, x_ref)
    w_ref[...] = -mm(x_ref[...], t_mm(u01[...], x0[...]))


def rows_kernel(loc_rows, pos, x0, x1, w, *rest):
    left, right, out = rest[:loc_rows], rest[loc_rows : 2 * loc_rows], rest[2 * loc_rows :]
    even_col = pos[1] % 2 == 0
    for a in range(loc_rows):
        l, r = left[a][...], right[a][...]
        b0, b1 = jnp.where(even_col, l, r), jnp.where(even_col, r, l)
        out[2 * a][...] = mm_t(b0, x0[...], HIGH)
        out[2 * a + 1][...] = mm_t(b0, w[...], HIGH) + mm_t(b1, x1[...], HIGH)


def last_kernel(
    loc_rows, loc_cols, pos, own, mine_a, mine_b, other_a, other_b, u0, x0, u1, x1, w, *rest
):
    prows, out = rest[: 2 * loc_rows], rest[2 * loc_rows]
    stride = 2 * loc_cols
    even = pos[0] % 2 == 0

    def top_tile(a, b, start):
        halves = [
            jnp.concatenate(
                [ref[pl.ds(start + k, HALF, stride=stride), :] for k in (0, 1)], axis=1
            )
            for ref in (a, b)
        ]
        return jnp.concatenate(halves, axis=0)

    for b in range(loc_cols):
        tile_col = pos[1] + b * pos[3]
        e, o = top_tile(mine_a, mine_b, 2 * b), top_tile(other_a, other_b, 2 * b)
        d0, d1 = jnp.where(even, e, o), jnp.where(even, o, e)
        q0 = mm(x0[...], d0, HIGH)
        q1 = mm(w[...], d0, HIGH) + mm(x1[...], d1, HIGH)
        for a in range(loc_rows):
            tile_row = pos[0] + a * pos[2]
            start = a * NB * stride + 2 * b

            def put(value, start=start):
                out[pl.ds(start, NB, stride=stride), :] = value[:, :HALF]
                out[pl.ds(start + 1, NB, stride=stride), :] = value[:, HALF:]

            @pl.when(tile_row < tile_col)
            def _():
                put(jnp.zeros((NB, NB), jnp.float32))

            @pl.when((tile_row >= tile_col) & (tile_col >= 2))
            def _():
                put(
                    tile_from(own, start, stride)
                    - (mm(prows[2 * a][...], q0, HIGH) + mm(prows[2 * a + 1][...], q1, HIGH))
                )

            if b == 0:

                @pl.when((tile_row > 0) & (tile_col == 0))
                def _():
                    put(prows[2 * a][...])

                @pl.when((tile_row > 1) & (tile_col == 1))
                def _():
                    put(prows[2 * a + 1][...])

                if a == 0:

                    @pl.when((tile_row == 0) & (tile_col == 0))
                    def _():
                        put(u0[...].T)

                    @pl.when((tile_row == 1) & (tile_col == 1))
                    def _():
                        put(u1[...].T)


VMEM = pl.BlockSpec(memory_space=pltpu.VMEM)
SMEM = pl.BlockSpec(memory_space=pltpu.SMEM)


def shape(*dims):
    return jax.ShapeDtypeStruct(dims, jnp.float32)


def call(kernel, out_shape, flops, *args, smem=0, vmem=16):
    return pl.pallas_call(
        kernel,
        out_shape=out_shape,
        in_specs=[SMEM] * smem + [VMEM] * (len(args) - smem),
        out_specs=jax.tree.map(lambda _: VMEM, out_shape),
        compiler_params=pltpu.CompilerParams(vmem_limit_bytes=vmem * 2**20),
        cost_estimate=pl.CostEstimate(flops=flops, bytes_accessed=2**22, transcendentals=0),
    )(*args)


def on_device(n_row, n_col, trailing_in):
    row = lax.axis_index("row")
    col = lax.axis_index("col")
    loc_rows, _, _, loc_cols, _, _ = trailing_in.shape
    stride = 2 * loc_cols
    chips = n_row // 2
    chip = row // 2
    own = trailing_in.reshape(loc_rows * NB * stride, HALF)
    pos = jnp.stack([row, col, jnp.int32(n_row), jnp.int32(n_col)]).astype(jnp.int32)
    row_bits = [1 << k for k in range(1, (n_row - 1).bit_length())]
    col_bits = [1 << k for k in range(1, (n_col - 1).bit_length())][::-1]
    after = lax.optimization_barrier

    def swap(value, axis, bits):
        size = n_row if axis == "row" else n_col
        return lax.ppermute(value, axis, [(i, i ^ bits) for i in range(size)])

    def pick(index, values):
        out = values[0]
        for k, value in enumerate(values[1:], 1):
            out = jnp.where(index == k, value, out)
        return out

    def spread(value, axis, bit, got=None):
        got = swap(value, axis, bit) if got is None else got
        return jnp.where((row if axis == "row" else col) & bit != 0, got, value)

    half = HALF * stride
    top_a, top_b, *left = call(
        functools.partial(pack_kernel, loc_rows, loc_cols),
        [shape(half, HALF), shape(half, HALF)] + [shape(NB, NB)] * loc_rows,
        10**8,
        own,
    )

    size = NB // chips
    pieces = [left[0][k * size : (k + 1) * size] for k in range(chips)]
    piece = pick(chip, [pieces[0]] + [swap(pieces[k], "row", 2 * k) for k in range(1, chips)])
    along = [piece] + [swap(piece, "col", k) for k in range(1, n_col)]
    pair = jnp.concatenate([pick(col, along), pick(col ^ 1, along)], axis=0)
    got = [swap(pair, "row", 2 * k) for k in range(1, chips)]

    left[0], got[0] = after((left[0], got[0]))
    got_left = swap(left[0], "col", col_bits[-1]) if len(col_bits) == 1 else None
    got = [pair] + got
    lead = [
        jnp.concatenate(
            [pick(chip ^ k, got)[j * size : (j + 1) * size] for k in range(chips)], axis=0
        )
        for j in (0, 1)
    ]
    other = swap(jnp.where(row % 2 == 0, lead[0], lead[1]), "row", 1)
    top_a, top_b, lead[0] = after((top_a, top_b, lead[0]))
    got_a = swap(top_a, "row", row_bits[0])
    got_b = swap(top_b, "row", row_bits[-1])

    u0, x0 = call(first_kernel, [shape(NB, NB)] * 2, 10**10, pos, lead[0], other, smem=1)
    got_left, got_a, got_b, lead[1], x0 = after((got_left, got_a, got_b, lead[1], x0))
    other_next = swap(lead[1], "row", 1)

    for first, second in zip(row_bits, row_bits[::-1]):
        top_a, top_b = spread(top_a, "row", first, got_a), spread(top_b, "row", second, got_b)
        got_a = got_b = None
    for bit in col_bits:
        left[0] = spread(left[0], "col", bit, got_left)
    right = [swap(left[0], "col", 1)]
    for a in range(1, loc_rows):
        left[a], x0 = after((left[a], x0))
        for bit in col_bits:
            left[a] = spread(left[a], "col", bit)

    u01, u_half, x_half, rest = call(
        second_kernel,
        [shape(NB, NB), shape(NB, HALF), shape(HALF, HALF), shape(HALF, HALF)],
        5 * 10**9,
        pos, x0, lead[0], lead[1], other, other_next,
        smem=1,
    )
    left, rest = after((left, rest))
    right += [swap(left[a], "col", 1) for a in range(1, loc_rows)]
    u1, x1, w = call(
        third_kernel, [shape(NB, NB)] * 3, 5 * 10**9, x0, u01, u_half, x_half, rest
    )
    top_a, top_b, right, x1 = after((top_a, top_b, right, x1))
    other_a, other_b = swap(top_a, "row", 1), swap(top_b, "row", 1)
    prows = call(
        functools.partial(rows_kernel, loc_rows),
        [shape(NB, NB)] * (2 * loc_rows),
        2 * 10**9,
        pos, x0, x1, w, *left, *right,
        smem=1,
    )
    out = call(
        functools.partial(last_kernel, loc_rows, loc_cols),
        shape(*own.shape),
        3 * 10**9,
        pos, own, top_a, top_b, other_a, other_b, u0, x0, u1, x1, w, *prows,
        smem=1,
        vmem=24,
    )
    return out.reshape(trailing_in.shape)


def solution(mesh):
    return jax.shard_map(
        functools.partial(on_device, mesh.shape["row"], mesh.shape["col"]),
        mesh=mesh,
        in_specs=(P(None, "row", None, None, "col", None),),
        out_specs=P(None, "row", None, None, "col", None),
        check_vma=False,
    )
```

profile of v0, /device:TPU:0, one launch (start us, length us, event | category | flops | bytes accessed | tf_op | source)
XLA Modules:
  0.0 74.8 jit_solution(8069036642072195201)
XLA Ops:
  0.0 1.6 %copy-done = f32[2,1,256,4,1,256]{5,4,3,2,1,0:T(1,128)S(1)} copy-done((f32[2,1,256,4,1,256]{5,4,3,2,1,0:T(1,128)S(1)}, f32[2,1,256,4,1,256]{5,4,3,2,1,0:T(1,128)}, u32[]{:S(2)}) %copy-start) | copy-done | bytes 2097176
  1.8 3.0 %collective-permute-start.2 = (f32[64,256]{1,0:T(8,128)S(1)}, f32[64,256]{1,0:T(8,128)S(1)}, u32[]{:S(2)}, u32[]{:S(2)}) collective-permute-start(f32[64,256]{1,0:T(8,128)S(1)} %get-tuple-element.87), channel_id=1, source_target_pairs={{0,8},{4,12},{8,0},{12,4},{16,24},{20,28},{24,16},{28,20},{1,9},{5... | collective-permute-start | bytes 196616 | tf_op jit(solution)/shard_map/ppermute | solution.py:290
  4.8 1.5 %collective-permute-start.1 = (f32[64,256]{1,0:T(8,128)S(1)}, f32[64,256]{1,0:T(8,128)S(1)}, u32[]{:S(2)}, u32[]{:S(2)}) collective-permute-start(f32[64,256]{1,0:T(8,128)S(1)} %get-tuple-element.88), channel_id=1, source_target_pairs={{0,16},{4,20},{8,24},{12,28},{16,0},{20,4},{24,8},{28,12},{1,17},{... | collective-permute-start | bytes 196616 | tf_op jit(solution)/shard_map/ppermute | solution.py:290
  6.3 0.8 %collective-permute-done.2 = f32[64,256]{1,0:T(8,128)S(1)} collective-permute-done((f32[64,256]{1,0:T(8,128)S(1)}, f32[64,256]{1,0:T(8,128)S(1)}, u32[]{:S(2)}, u32[]{:S(2)}) %collective-permute-start.2) | collective-permute-done | bytes 65568 | tf_op jit(solution)/shard_map/ppermute | solution.py:290
  7.1 1.9 %collective-permute-done.1 = f32[64,256]{1,0:T(8,128)S(1)} collective-permute-done((f32[64,256]{1,0:T(8,128)S(1)}, f32[64,256]{1,0:T(8,128)S(1)}, u32[]{:S(2)}, u32[]{:S(2)}) %collective-permute-start.1) | collective-permute-done | bytes 65568 | tf_op jit(solution)/shard_map/ppermute | solution.py:290
  9.1 2.4 %collective-permute-done = f32[64,256]{1,0:T(8,128)S(1)} collective-permute-done((f32[64,256]{1,0:T(8,128)S(1)}, f32[64,256]{1,0:T(8,128)S(1)}, u32[]{:S(2)}, u32[]{:S(2)}) %collective-permute-start) | collective-permute-done | bytes 65568 | tf_op jit(solution)/shard_map/ppermute | solution.py:290
  11.5 1.6 %collective-permute-start.5 = (f32[64,256]{1,0:T(8,128)S(1)}, f32[64,256]{1,0:T(8,128)S(1)}, u32[]{:S(2)}, u32[]{:S(2)}) collective-permute-start(f32[64,256]{1,0:T(8,128)S(1)} %select_select_fusion.6), channel_id=1, source_target_pairs={{0,1},{1,0},{2,3},{3,2},{4,5},{5,4},{6,7},{7,6},{8,9},{9,8},{10,11... | collective-permute-start | bytes 196616 | tf_op jit(solution)/shard_map/ppermute | solution.py:290
  13.1 2.6 %collective-permute-start.4 = (f32[64,256]{1,0:T(8,128)S(1)}, f32[64,256]{1,0:T(8,128)S(1)}, u32[]{:S(2)}, u32[]{:S(2)}) collective-permute-start(f32[64,256]{1,0:T(8,128)S(1)} %select_select_fusion.6), channel_id=1, source_target_pairs={{0,2},{1,3},{2,0},{3,1},{4,6},{5,7},{6,4},{7,5},{8,10},{9,11},{10,... | collective-permute-start | bytes 196616 | tf_op jit(solution)/shard_map/ppermute | solution.py:290
  16.0 3.8 %collective-permute-done.4 = f32[64,256]{1,0:T(8,128)S(1)} collective-permute-done((f32[64,256]{1,0:T(8,128)S(1)}, f32[64,256]{1,0:T(8,128)S(1)}, u32[]{:S(2)}, u32[]{:S(2)}) %collective-permute-start.4) | collective-permute-done | bytes 65568 | tf_op jit(solution)/shard_map/ppermute | solution.py:290
  19.7 2.1 %collective-permute-done.3 = f32[64,256]{1,0:T(8,128)S(1)} collective-permute-done((f32[64,256]{1,0:T(8,128)S(1)}, f32[64,256]{1,0:T(8,128)S(1)}, u32[]{:S(2)}, u32[]{:S(2)}) %collective-permute-start.3) | collective-permute-done | bytes 65568 | tf_op jit(solution)/shard_map/ppermute | solution.py:290
  21.8 0.6 collective-permute-start.6
  22.9 2.4 %collective-permute-start.8 = (f32[128,256]{1,0:T(8,128)S(1)}, f32[128,256]{1,0:T(8,128)S(1)}, u32[]{:S(2)}, u32[]{:S(2)}) collective-permute-start(f32[128,256]{1,0:T(8,128)S(1)} %pad_maximum_fusion.2), channel_id=1, source_target_pairs={{0,24},{4,28},{8,16},{12,20},{16,8},{20,12},{24,0},{28,4},{1,25},{... | collective-permute-start | bytes 393224 | tf_op jit(solution)/shard_map/ppermute | solution.py:290
  25.4 1.5 %collective-permute-done.6 = f32[128,256]{1,0:T(8,128)S(1)} collective-permute-done((f32[128,256]{1,0:T(8,128)S(1)}, f32[128,256]{1,0:T(8,128)S(1)}, u32[]{:S(2)}, u32[]{:S(2)}) %collective-permute-start.6) | collective-permute-done | bytes 131104 | tf_op jit(solution)/shard_map/ppermute | solution.py:290
  26.9 0.5 collective-permute-done.9
  27.4 1.4 %collective-permute-done.8 = f32[128,256]{1,0:T(8,128)S(1)} collective-permute-done((f32[128,256]{1,0:T(8,128)S(1)}, f32[128,256]{1,0:T(8,128)S(1)}, u32[]{:S(2)}, u32[]{:S(2)}) %collective-permute-start.8) | collective-permute-done | bytes 131104 | tf_op jit(solution)/shard_map/ppermute | solution.py:290
  29.2 0.7 collective-permute-start.7
  29.9 1.0 %collective-permute-start.10 = (f32[1024,128]{1,0:T(8,128)S(1)}, f32[1024,128]{1,0:T(8,128)S(1)}, u32[]{:S(2)}, u32[]{:S(2)}) collective-permute-start(f32[1024,128]{1,0:T(8,128)S(1)} %get-tuple-element.47), channel_id=1, source_target_pairs={{0,8},{4,12},{8,0},{12,4},{16,24},{20,28},{24,16},{28,20},{1,9},{5... | collective-permute-start | bytes 1572872 | tf_op jit(solution)/shard_map/ppermute | solution.py:290
  30.9 1.5 %collective-permute-start.11 = (f32[1024,128]{1,0:T(8,128)S(1)}, f32[1024,128]{1,0:T(8,128)S(1)}, u32[]{:S(2)}, u32[]{:S(2)}) collective-permute-start(f32[1024,128]{1,0:T(8,128)S(1)} %get-tuple-element.48), channel_id=1, source_target_pairs={{0,16},{4,20},{8,24},{12,28},{16,0},{20,4},{24,8},{28,12},{1,17},{... | collective-permute-start | bytes 1572872 | tf_op jit(solution)/shard_map/ppermute | solution.py:290
  32.4 8.4 %shard_map.18 = (f32[256,256]{1,0:T(8,128)S(1)}, f32[256,256]{1,0:T(8,128)S(1)}) custom-call(s32[4]{0:T(128)S(1)} %pad_add_fusion.pos, f32[256,256]{1,0:T(8,128)S(1)} %get-tuple-element.49.mine.mine0, f32[256,256]{1,0:T(8,128)S(1)} %collective-permute-done.12.other.other0), custom_call_target="tpu_custom_call" | custom-call | flops 10000000000 | bytes 4194304 | tf_op jit(solution)/shard_map/pallas_call | solution.py:265
  40.8 2.2 %collective-permute-done.7 = f32[256,256]{1,0:T(8,128)S(1)} collective-permute-done((f32[256,256]{1,0:T(8,128)S(1)}, f32[256,256]{1,0:T(8,128)S(1)}, u32[]{:S(2)}, u32[]{:S(2)}) %collective-permute-start.7) | collective-permute-done | bytes 262176 | tf_op jit(solution)/shard_map/ppermute | solution.py:290
  43.0 0.9 %collective-permute-done.10 = f32[1024,128]{1,0:T(8,128)S(1)} collective-permute-done((f32[1024,128]{1,0:T(8,128)S(1)}, f32[1024,128]{1,0:T(8,128)S(1)}, u32[]{:S(2)}, u32[]{:S(2)}) %collective-permute-start.10) | collective-permute-done | bytes 524320 | tf_op jit(solution)/shard_map/ppermute | solution.py:290
  43.9 0.9 %collective-permute-done.11 = f32[1024,128]{1,0:T(8,128)S(1)} collective-permute-done((f32[1024,128]{1,0:T(8,128)S(1)}, f32[1024,128]{1,0:T(8,128)S(1)}, u32[]{:S(2)}, u32[]{:S(2)}) %collective-permute-start.11) | collective-permute-done | bytes 524320 | tf_op jit(solution)/shard_map/ppermute | solution.py:290
  44.8 2.6 %collective-permute-start.16 = (f32[256,256]{1,0:T(8,128)S(1)}, f32[256,256]{1,0:T(8,128)S(1)}, u32[]{:S(2)}, u32[]{:S(2)}) collective-permute-start(f32[256,256]{1,0:T(8,128)S(1)} %get-tuple-element.56), channel_id=1, source_target_pairs={{0,2},{1,3},{2,0},{3,1},{4,6},{5,7},{6,4},{7,5},{8,10},{9,11},{10,... | collective-permute-start | bytes 786440 | tf_op jit(solution)/shard_map/ppermute | solution.py:290
  47.6 0.6 collective-permute-start.14
  48.3 1.6 %collective-permute-start.13 = (f32[1024,128]{1,0:T(8,128)S(1)}, f32[1024,128]{1,0:T(8,128)S(1)}, u32[]{:S(2)}, u32[]{:S(2)}) collective-permute-start(f32[1024,128]{1,0:T(8,128)S(1)} %broadcast_select_fusion.1), channel_id=1, source_target_pairs={{0,16},{4,20},{8,24},{12,28},{16,0},{20,4},{24,8},{28,12},{1,17},{... | collective-permute-start | bytes 1572872 | tf_op jit(solution)/shard_map/ppermute | solution.py:290
  49.9 5.9 %shard_map.19 = (f32[256,256]{1,0:T(8,128)S(1)}, f32[256,128]{1,0:T(8,128)S(1)}, f32[128,128]{1,0:T(8,128)S(1)}, f32[128,128]{1,0:T(8,128)S(1)}) custom-call(s32[4]{0:T(128)S(1)} %pad_add_fusion.pos, f32[256,256]{1,0:T(8,128)S(1)} %get-tuple-element.57.x0, f32[256,256]{1,0:T(8,128)S(1)} %get-tuple-element.49.mine.mine0, ...), custom_call_target="tpu_custom_call" | custom-call | flops 5000000000 | bytes 4194304 | tf_op jit(solution)/shard_map/pallas_call | solution.py:265
  55.8 3.1 %collective-permute-done.16 = f32[256,256]{1,0:T(8,128)S(1)} collective-permute-done((f32[256,256]{1,0:T(8,128)S(1)}, f32[256,256]{1,0:T(8,128)S(1)}, u32[]{:S(2)}, u32[]{:S(2)}) %collective-permute-start.16) | collective-permute-done | bytes 262176 | tf_op jit(solution)/shard_map/ppermute | solution.py:290
  58.9 5.1 %shard_map.20 = (f32[256,256]{1,0:T(8,128)S(1)}, f32[256,256]{1,0:T(8,128)S(1)}, f32[256,256]{1,0:T(8,128)S(1)}) custom-call(f32[256,256]{1,0:T(8,128)S(1)} %get-tuple-element.57.x0, f32[256,256]{1,0:T(8,128)S(1)} %get-tuple-element.61.u01, f32[256,128]{1,0:T(8,128)S(1)} %get-tuple-element.62.ua, f32[128,128]{1,0:T(8,128)S(1)} %get-tuple-element.63.xa, ...), custom_call_target="tpu_custom_call" | custom-call | flops 5000000000 | bytes 4194304 | tf_op jit(solution)/shard_map/pallas_call | solution.py:265
  64.2 2.5 %collective-permute-done.18.rest_3_ = f32[256,256]{1,0:T(8,128)S(1)} collective-permute-done((f32[256,256]{1,0:T(8,128)S(1)}, f32[256,256]{1,0:T(8,128)S(1)}, u32[]{:S(2)}, u32[]{:S(2)}) %collective-permute-start.18) | collective-permute-done | bytes 262176 | tf_op jit(solution)/shard_map/ppermute | solution.py:290
  67.2 1.4 %shard_map.21 = (f32[256,256]{1,0:T(8,128)S(1)}, f32[256,256]{1,0:T(8,128)S(1)}, f32[256,256]{1,0:T(8,128)S(1)}, f32[256,256]{1,0:T(8,128)S(1)}) custom-call(s32[4]{0:T(128)S(1)} %pad_add_fusion.pos, f32[256,256]{1,0:T(8,128)S(1)} %get-tuple-element.57.x0, f32[256,256]{1,0:T(8,128)S(1)} %get-tuple-element.70.x1, f32[256,256]{1,0:T(8,128)S(1)} %get-tuple-element.71.w, ...), custom_call_target="tpu_custom_call" | custom-call | flops 2000000000 | bytes 4194304 | tf_op jit(solution)/shard_map/pallas_call | solution.py:265
  68.7 0.7 collective-permute-done.20.other_b
  69.4 5.4 %shard_map.22 = f32[4096,128]{1,0:T(8,128)} custom-call(s32[4]{0:T(128)S(1)} %pad_add_fusion.pos, f32[4096,128]{1,0:T(8,128)S(1)} %bitcast.5, f32[1024,128]{1,0:T(8,128)S(1)} %broadcast_select_fusion.3.mine_a, f32[1024,128]{1,0:T(8,128)S(1)} %broadcast_select_fusion.mine_b, f32[1024,128]{1,0:T(8,128)S(1)} %collective-permute-done.19.other_a, ...), custom_call_target="tpu_custom_call" | custom-call | flops 3000000000 | bytes 4194304 | tf_op jit(solution)/shard_map/pallas_call | solution.py:265
  (36 shorter events, 2.4 us)
Async XLA Ops:
  0.0 1.6 %copy-start = (f32[2,1,256,4,1,256]{5,4,3,2,1,0:T(1,128)S(1)}, f32[2,1,256,4,1,256]{5,4,3,2,1,0:T(1,128)}, u32[]{:S(2)}) copy-start(f32[2,1,256,4,1,256]{5,4,3,2,1,0:T(1,128)} %param.1) | copy-start | bytes 6291460
  1.8 5.4 %collective-permute-start.2 = (f32[64,256]{1,0:T(8,128)S(1)}, f32[64,256]{1,0:T(8,128)S(1)}, u32[]{:S(2)}, u32[]{:S(2)}) collective-permute-start(f32[64,256]{1,0:T(8,128)S(1)} %get-tuple-element.87), channel_id=1, source_target_pairs={{0,8},{4,12},{8,0},{12,4},{16,24},{20,28},{24,16},{28,20},{1,9},{5... | collective-permute-start | bytes 196616 | tf_op jit(solution)/shard_map/ppermute | solution.py:290
  4.8 4.3 %collective-permute-start.1 = (f32[64,256]{1,0:T(8,128)S(1)}, f32[64,256]{1,0:T(8,128)S(1)}, u32[]{:S(2)}, u32[]{:S(2)}) collective-permute-start(f32[64,256]{1,0:T(8,128)S(1)} %get-tuple-element.88), channel_id=1, source_target_pairs={{0,16},{4,20},{8,24},{12,28},{16,0},{20,4},{24,8},{28,12},{1,17},{... | collective-permute-start | bytes 196616 | tf_op jit(solution)/shard_map/ppermute | solution.py:290
  6.3 5.2 %collective-permute-start = (f32[64,256]{1,0:T(8,128)S(1)}, f32[64,256]{1,0:T(8,128)S(1)}, u32[]{:S(2)}, u32[]{:S(2)}) collective-permute-start(f32[64,256]{1,0:T(8,128)S(1)} %get-tuple-element.89), channel_id=1, source_target_pairs={{0,24},{4,28},{8,16},{12,20},{16,8},{20,12},{24,0},{28,4},{1,25},{... | collective-permute-start | bytes 196616 | tf_op jit(solution)/shard_map/ppermute | solution.py:290
  11.5 4.5 %collective-permute-start.5 = (f32[64,256]{1,0:T(8,128)S(1)}, f32[64,256]{1,0:T(8,128)S(1)}, u32[]{:S(2)}, u32[]{:S(2)}) collective-permute-start(f32[64,256]{1,0:T(8,128)S(1)} %select_select_fusion.6), channel_id=1, source_target_pairs={{0,1},{1,0},{2,3},{3,2},{4,5},{5,4},{6,7},{7,6},{8,9},{9,8},{10,11... | collective-permute-start | bytes 196616 | tf_op jit(solution)/shard_map/ppermute | solution.py:290
  13.1 6.6 %collective-permute-start.4 = (f32[64,256]{1,0:T(8,128)S(1)}, f32[64,256]{1,0:T(8,128)S(1)}, u32[]{:S(2)}, u32[]{:S(2)}) collective-permute-start(f32[64,256]{1,0:T(8,128)S(1)} %select_select_fusion.6), channel_id=1, source_target_pairs={{0,2},{1,3},{2,0},{3,1},{4,6},{5,7},{6,4},{7,5},{8,10},{9,11},{10,... | collective-permute-start | bytes 196616 | tf_op jit(solution)/shard_map/ppermute | solution.py:290
  15.7 6.1 %collective-permute-start.3 = (f32[64,256]{1,0:T(8,128)S(1)}, f32[64,256]{1,0:T(8,128)S(1)}, u32[]{:S(2)}, u32[]{:S(2)}) collective-permute-start(f32[64,256]{1,0:T(8,128)S(1)} %select_select_fusion.6), channel_id=1, source_target_pairs={{0,3},{1,2},{2,1},{3,0},{4,7},{5,6},{6,5},{7,4},{8,11},{9,10},{10,... | collective-permute-start | bytes 196616 | tf_op jit(solution)/shard_map/ppermute | solution.py:290
  21.8 5.0 %collective-permute-start.6 = (f32[128,256]{1,0:T(8,128)S(1)}, f32[128,256]{1,0:T(8,128)S(1)}, u32[]{:S(2)}, u32[]{:S(2)}) collective-permute-start(f32[128,256]{1,0:T(8,128)S(1)} %pad_maximum_fusion.2), channel_id=1, source_target_pairs={{0,8},{4,12},{8,0},{12,4},{16,24},{20,28},{24,16},{28,20},{1,9},{5... | collective-permute-start | bytes 393224 | tf_op jit(solution)/shard_map/ppermute | solution.py:290
  22.4 5.0 %collective-permute-start.9 = (f32[128,256]{1,0:T(8,128)S(1)}, f32[128,256]{1,0:T(8,128)S(1)}, u32[]{:S(2)}, u32[]{:S(2)}) collective-permute-start(f32[128,256]{1,0:T(8,128)S(1)} %pad_maximum_fusion.2), channel_id=1, source_target_pairs={{0,16},{4,20},{8,24},{12,28},{16,0},{20,4},{24,8},{28,12},{1,17},{... | collective-permute-start | bytes 393224 | tf_op jit(solution)/shard_map/ppermute | solution.py:290
  22.9 5.9 %collective-permute-start.8 = (f32[128,256]{1,0:T(8,128)S(1)}, f32[128,256]{1,0:T(8,128)S(1)}, u32[]{:S(2)}, u32[]{:S(2)}) collective-permute-start(f32[128,256]{1,0:T(8,128)S(1)} %pad_maximum_fusion.2), channel_id=1, source_target_pairs={{0,24},{4,28},{8,16},{12,20},{16,8},{20,12},{24,0},{28,4},{1,25},{... | collective-permute-start | bytes 393224 | tf_op jit(solution)/shard_map/ppermute | solution.py:290
  29.0 3.4 %collective-permute-start.12 = (f32[256,256]{1,0:T(8,128)S(1)}, f32[256,256]{1,0:T(8,128)S(1)}, u32[]{:S(2)}, u32[]{:S(2)}) collective-permute-start(f32[256,256]{1,0:T(8,128)S(1)} %get-tuple-element.82), channel_id=1, source_target_pairs={{0,4},{4,0},{8,12},{12,8},{16,20},{20,16},{24,28},{28,24},{1,5},{5... | collective-permute-start | bytes 786440 | tf_op jit(solution)/shard_map/ppermute | solution.py:290
  29.2 13.8 %collective-permute-start.7 = (f32[256,256]{1,0:T(8,128)S(1)}, f32[256,256]{1,0:T(8,128)S(1)}, u32[]{:S(2)}, u32[]{:S(2)}) collective-permute-start(f32[256,256]{1,0:T(8,128)S(1)} %get-tuple-element.43), channel_id=1, source_target_pairs={{0,2},{1,3},{2,0},{3,1},{4,6},{5,7},{6,4},{7,5},{8,10},{9,11},{10,... | collective-permute-start | bytes 786440 | tf_op jit(solution)/shard_map/ppermute | solution.py:290
  29.9 14.0 %collective-permute-start.10 = (f32[1024,128]{1,0:T(8,128)S(1)}, f32[1024,128]{1,0:T(8,128)S(1)}, u32[]{:S(2)}, u32[]{:S(2)}) collective-permute-start(f32[1024,128]{1,0:T(8,128)S(1)} %get-tuple-element.47), channel_id=1, source_target_pairs={{0,8},{4,12},{8,0},{12,4},{16,24},{20,28},{24,16},{28,20},{1,9},{5... | collective-permute-start | bytes 1572872 | tf_op jit(solution)/shard_map/ppermute | solution.py:290
  30.9 13.9 %collective-permute-start.11 = (f32[1024,128]{1,0:T(8,128)S(1)}, f32[1024,128]{1,0:T(8,128)S(1)}, u32[]{:S(2)}, u32[]{:S(2)}) collective-permute-start(f32[1024,128]{1,0:T(8,128)S(1)} %get-tuple-element.48), channel_id=1, source_target_pairs={{0,16},{4,20},{8,24},{12,28},{16,0},{20,4},{24,8},{28,12},{1,17},{... | collective-permute-start | bytes 1572872 | tf_op jit(solution)/shard_map/ppermute | solution.py:290
  44.8 14.0 %collective-permute-start.16 = (f32[256,256]{1,0:T(8,128)S(1)}, f32[256,256]{1,0:T(8,128)S(1)}, u32[]{:S(2)}, u32[]{:S(2)}) collective-permute-start(f32[256,256]{1,0:T(8,128)S(1)} %get-tuple-element.56), channel_id=1, source_target_pairs={{0,2},{1,3},{2,0},{3,1},{4,6},{5,7},{6,4},{7,5},{8,10},{9,11},{10,... | collective-permute-start | bytes 786440 | tf_op jit(solution)/shard_map/ppermute | solution.py:290
  47.4 16.8 %collective-permute-start.15 = (f32[256,256]{1,0:T(8,128)S(1)}, f32[256,256]{1,0:T(8,128)S(1)}, u32[]{:S(2)}, u32[]{:S(2)}) collective-permute-start(f32[256,256]{1,0:T(8,128)S(1)} %broadcast_select_fusion.5.rest_0_), channel_id=1, source_target_pairs={{0,1},{1,0},{2,3},{3,2},{4,5},{5,4},{6,7},{7,6},{8,9},{9,8},{10,11... | collective-permute-start | bytes 786440 | tf_op jit(solution)/shard_map/ppermute | solution.py:290
  47.5 2.4 %collective-permute-start.17 = (f32[256,256]{1,0:T(8,128)S(1)}, f32[256,256]{1,0:T(8,128)S(1)}, u32[]{:S(2)}, u32[]{:S(2)}) collective-permute-start(f32[256,256]{1,0:T(8,128)S(1)} %get-tuple-element.58.mine1), channel_id=1, source_target_pairs={{0,4},{4,0},{8,12},{12,8},{16,20},{20,16},{24,28},{28,24},{1,5},{5... | collective-permute-start | bytes 786440 | tf_op jit(solution)/shard_map/ppermute | solution.py:290
  47.6 16.4 %collective-permute-start.14 = (f32[1024,128]{1,0:T(8,128)S(1)}, f32[1024,128]{1,0:T(8,128)S(1)}, u32[]{:S(2)}, u32[]{:S(2)}) collective-permute-start(f32[1024,128]{1,0:T(8,128)S(1)} %broadcast_select_fusion.2), channel_id=1, source_target_pairs={{0,8},{4,12},{8,0},{12,4},{16,24},{20,28},{24,16},{28,20},{1,9},{5... | collective-permute-start | bytes 1572872 | tf_op jit(solution)/shard_map/ppermute | solution.py:290
  48.3 15.9 %collective-permute-start.13 = (f32[1024,128]{1,0:T(8,128)S(1)}, f32[1024,128]{1,0:T(8,128)S(1)}, u32[]{:S(2)}, u32[]{:S(2)}) collective-permute-start(f32[1024,128]{1,0:T(8,128)S(1)} %broadcast_select_fusion.1), channel_id=1, source_target_pairs={{0,16},{4,20},{8,24},{12,28},{16,0},{20,4},{24,8},{28,12},{1,17},{... | collective-permute-start | bytes 1572872 | tf_op jit(solution)/shard_map/ppermute | solution.py:290
  58.9 7.9 %collective-permute-start.18 = (f32[256,256]{1,0:T(8,128)S(1)}, f32[256,256]{1,0:T(8,128)S(1)}, u32[]{:S(2)}, u32[]{:S(2)}) collective-permute-start(f32[256,256]{1,0:T(8,128)S(1)} %broadcast_select_fusion.4.rest_1_), channel_id=1, source_target_pairs={{0,1},{1,0},{2,3},{3,2},{4,5},{5,4},{6,7},{7,6},{8,9},{9,8},{10,11... | collective-permute-start | bytes 786440 | tf_op jit(solution)/shard_map/ppermute | solution.py:290
  66.7 1.9 %collective-permute-start.19 = (f32[1024,128]{1,0:T(8,128)S(1)}, f32[1024,128]{1,0:T(8,128)S(1)}, u32[]{:S(2)}, u32[]{:S(2)}) collective-permute-start(f32[1024,128]{1,0:T(8,128)S(1)} %broadcast_select_fusion.3.mine_a), channel_id=1, source_target_pairs={{0,4},{4,0},{8,12},{12,8},{16,20},{20,16},{24,28},{28,24},{1,5},{5... | collective-permute-start | bytes 1572872 | tf_op jit(solution)/shard_map/ppermute | solution.py:290
  66.7 2.7 %collective-permute-start.20 = (f32[1024,128]{1,0:T(8,128)S(1)}, f32[1024,128]{1,0:T(8,128)S(1)}, u32[]{:S(2)}, u32[]{:S(2)}) collective-permute-start(f32[1024,128]{1,0:T(8,128)S(1)} %broadcast_select_fusion.mine_b), channel_id=1, source_target_pairs={{0,4},{4,0},{8,12},{12,8},{16,20},{20,16},{24,28},{28,24},{1,5},{5... | collective-permute-start | bytes 1572872 | tf_op jit(solution)/shard_map/ppermute | solution.py:290
  67.2 2.2 %copy-start.1 = (f32[2,1,256,4,1,256]{5,4,3,2,1,0:T(1,128)S(1)}, f32[2,1,256,4,1,256]{5,4,3,2,1,0:T(1,128)}, u32[]{:S(2)}) copy-start(f32[2,1,256,4,1,256]{5,4,3,2,1,0:T(1,128)} %param.1) | copy-start | bytes 6291460
where the time goes:
time: 74.9 us; the launch traced here: 74.8 us
  Pallas kernels  26.3 us (35%)
  waiting for transfers between devices  24.7 us (33%)
  starting transfers between devices  21.3 us (28%)
  local copies, waits for them, and re-layouts  1.65 us (2%)
    pallas_call x6, Pallas kernels, call(): pl.pallas_call(kernel, out_shape=out_shape, in_specs=[SMEM] * smem + [VME...  26.3 us
    ppermute x21, waiting for transfers between devices, swap(): return lax.ppermute(value, axis, [(i, i ^ bits) for i in range(size)])  24.7 us
    ppermute x21, starting transfers between devices, swap(): return lax.ppermute(value, axis, [(i, i ^ bits) for i in range(size)])  21.3 us
    unnamed x4, local copies, waits for them, and re-layouts  1.59 us
  transfers between devices with their start and end apart: 21, of which 14 were waited for; matrix products, arithmetic and copies ran while one was open for 1% of the time, Pallas kernels for 28%

commit v1 on v0

--- a/solution.py
+++ b/solution.py
@@ -155,48 +155,32 @@
     top_b[...] = own[half : 2 * half, :]
 
 
-def start_blocks(s, u_ref, x_ref, rest_ref):
-    u11, x11 = factor_half(s[:HALF, :HALF])
-    u12 = mm(x11, s[:HALF, HALF:])
-    u_ref[:HALF, :] = u11
-    u_ref[HALF:, :] = u12
-    x_ref[...] = x11
-    rest_ref[...] = s[HALF:, HALF:] - t_mm(u12, u12)
-
-
 def first_kernel(pos, mine, other, u_ref, x_ref):
     s = jnp.where(pos[0] % 2 == 0, mine[...], other[...])
     factor_blocks(s[:HALF, :HALF], s[:HALF, HALF:], s[HALF:, HALF:], u_ref, x_ref)
 
 
-def second_kernel(pos, x0, mine0, mine1, other0, other1, u01_ref, u_ref, x_ref, rest_ref):
+def second_kernel(pos, x0, mine0, mine1, other0, other1, u_ref, x_ref, w_ref):
     even = pos[0] % 2 == 0
     u01 = mm(x0[...], jnp.where(even, mine1[...], other1[...]))
-    u01_ref[...] = u01
-    start_blocks(jnp.where(even, other0[...], mine1[...]) - t_mm(u01, u01), u_ref, x_ref, rest_ref)
-
-
-def third_kernel(x0, u01, ua, xa, rest, u_ref, x_ref, w_ref):
-    finish_blocks(ua[:HALF, :], ua[HALF:, :], xa[...], rest[...], u_ref, x_ref)
-    w_ref[...] = -mm(x_ref[...], t_mm(u01[...], x0[...]))
-
-
-def rows_kernel(loc_rows, pos, x0, x1, w, *rest):
-    left, right, out = rest[:loc_rows], rest[loc_rows : 2 * loc_rows], rest[2 * loc_rows :]
+    s = jnp.where(even, other0[...], mine1[...]) - t_mm(u01, u01)
+    factor_blocks(s[:HALF, :HALF], s[:HALF, HALF:], s[HALF:, HALF:], u_ref, x_ref)
+    w_ref[...] = -mm(x_ref[...], t_mm(u01, x0[...]))
+
+
+def last_kernel(
+    loc_rows, loc_cols, pos, own, mine_a, mine_b, other_a, other_b, u0, x0, u1, x1, w, *rest
+):
+    left, right = rest[:loc_rows], rest[loc_rows : 2 * loc_rows]
+    out, prows = rest[2 * loc_rows :]
+    stride = 2 * loc_cols
+    even = pos[0] % 2 == 0
     even_col = pos[1] % 2 == 0
     for a in range(loc_rows):
         l, r = left[a][...], right[a][...]
         b0, b1 = jnp.where(even_col, l, r), jnp.where(even_col, r, l)
-        out[2 * a][...] = mm_t(b0, x0[...], HIGH)
-        out[2 * a + 1][...] = mm_t(b0, w[...], HIGH) + mm_t(b1, x1[...], HIGH)
-
-
-def last_kernel(
-    loc_rows, loc_cols, pos, own, mine_a, mine_b, other_a, other_b, u0, x0, u1, x1, w, *rest
-):
-    prows, out = rest[: 2 * loc_rows], rest[2 * loc_rows]
-    stride = 2 * loc_cols
-    even = pos[0] % 2 == 0
+        prows[2 * a] = mm_t(b0, x0[...], HIGH)
+        prows[2 * a + 1] = mm_t(b0, w[...], HIGH) + mm_t(b1, x1[...], HIGH)
 
     def top_tile(a, b, start):
         halves = [
@@ -229,18 +213,18 @@
             def _():
                 put(
                     tile_from(own, start, stride)
-                    - (mm(prows[2 * a][...], q0, HIGH) + mm(prows[2 * a + 1][...], q1, HIGH))
+                    - (mm(prows[2 * a], q0, HIGH) + mm(prows[2 * a + 1], q1, HIGH))
                 )
 
             if b == 0:
 
                 @pl.when((tile_row > 0) & (tile_col == 0))
                 def _():
-                    put(prows[2 * a][...])
+                    put(prows[2 * a])
 
                 @pl.when((tile_row > 1) & (tile_col == 1))
                 def _():
-                    put(prows[2 * a + 1][...])
+                    put(prows[2 * a + 1])
 
                 if a == 0:
 
@@ -261,12 +245,13 @@
     return jax.ShapeDtypeStruct(dims, jnp.float32)
 
 
-def call(kernel, out_shape, flops, *args, smem=0, vmem=16):
+def call(kernel, out_shape, flops, *args, smem=0, vmem=16, scratch=()):
     return pl.pallas_call(
         kernel,
         out_shape=out_shape,
         in_specs=[SMEM] * smem + [VMEM] * (len(args) - smem),
         out_specs=jax.tree.map(lambda _: VMEM, out_shape),
+        scratch_shapes=list(scratch),
         compiler_params=pltpu.CompilerParams(vmem_limit_bytes=vmem * 2**20),
         cost_estimate=pl.CostEstimate(flops=flops, bytes_accessed=2**22, transcendentals=0),
     )(*args)
@@ -295,8 +280,7 @@
             out = jnp.where(index == k, value, out)
         return out
 
-    def spread(value, axis, bit, got=None):
-        got = swap(value, axis, bit) if got is None else got
+    def settle(value, axis, bit, got):
         return jnp.where((row if axis == "row" else col) & bit != 0, got, value)
 
     half = HALF * stride
@@ -311,66 +295,58 @@
     pieces = [left[0][k * size : (k + 1) * size] for k in range(chips)]
     piece = pick(chip, [pieces[0]] + [swap(pieces[k], "row", 2 * k) for k in range(1, chips)])
     along = [piece] + [swap(piece, "col", k) for k in range(1, n_col)]
+    top_a, top_b, along[1] = after((top_a, top_b, along[1]))
+    got_a, got_b = swap(top_a, "row", row_bits[0]), swap(top_b, "row", row_bits[-1])
     pair = jnp.concatenate([pick(col, along), pick(col ^ 1, along)], axis=0)
-    got = [swap(pair, "row", 2 * k) for k in range(1, chips)]
-
-    left[0], got[0] = after((left[0], got[0]))
-    got_left = swap(left[0], "col", col_bits[-1]) if len(col_bits) == 1 else None
-    got = [pair] + got
+    got = [pair] + [swap(pair, "row", 2 * k) for k in range(1, chips)]
+    left[0], got[1] = after((left[0], got[1]))
+    got_left = [swap(left[0], "col", col_bits[0])]
+    got_a, got_b, got = after((got_a, got_b, got))
     lead = [
         jnp.concatenate(
             [pick(chip ^ k, got)[j * size : (j + 1) * size] for k in range(chips)], axis=0
         )
         for j in (0, 1)
     ]
-    other = swap(jnp.where(row % 2 == 0, lead[0], lead[1]), "row", 1)
-    top_a, top_b, lead[0] = after((top_a, top_b, lead[0]))
-    got_a = swap(top_a, "row", row_bits[0])
-    got_b = swap(top_b, "row", row_bits[-1])
-
-    u0, x0 = call(first_kernel, [shape(NB, NB)] * 2, 10**10, pos, lead[0], other, smem=1)
-    got_left, got_a, got_b, lead[1], x0 = after((got_left, got_a, got_b, lead[1], x0))
-    other_next = swap(lead[1], "row", 1)
-
-    for first, second in zip(row_bits, row_bits[::-1]):
-        top_a, top_b = spread(top_a, "row", first, got_a), spread(top_b, "row", second, got_b)
-        got_a = got_b = None
-    for bit in col_bits:
-        left[0] = spread(left[0], "col", bit, got_left)
-    right = [swap(left[0], "col", 1)]
-    for a in range(1, loc_rows):
-        left[a], x0 = after((left[a], x0))
-        for bit in col_bits:
-            left[a] = spread(left[a], "col", bit)
-
-    u01, u_half, x_half, rest = call(
+    lead_other = swap(jnp.where(row % 2 == 0, lead[0], lead[1]), "row", 1)
+
+    left, lead[0] = after((left, lead[0]))
+    top_a = settle(top_a, "row", row_bits[0], got_a)
+    top_b = settle(top_b, "row", row_bits[-1], got_b)
+    for first, second in zip(row_bits[1:-1], row_bits[-2:0:-1]):
+        top_a = settle(top_a, "row", first, swap(top_a, "row", first))
+        top_b = settle(top_b, "row", second, swap(top_b, "row", second))
+    got_a, got_b = swap(top_a, "row", row_bits[-1]), swap(top_b, "row", row_bits[0])
+    got_left += [swap(left[a], "col", col_bits[0]) for a in range(1, loc_rows)]
+    u0, x0 = call(first_kernel, [shape(NB, NB)] * 2, 10**10, pos, lead[0], lead_other, smem=1)
+
+    got_a, got_b, got_left, lead[1], x0 = after((got_a, got_b, got_left, lead[1], x0))
+    lead_next = swap(lead[1], "row", 1)
+    right = []
+    for a in range(loc_rows):
+        left[a] = settle(left[a], "col", col_bits[0], got_left[a])
+        for bit in col_bits[1:]:
+            left[a] = settle(left[a], "col", bit, swap(left[a], "col", bit))
+        right.append(swap(left[a], "col", 1))
+    top_a = settle(top_a, "row", row_bits[-1], got_a)
+    top_b = settle(top_b, "row", row_bits[0], got_b)
+    other_a, other_b = swap(top_a, "row", 1), swap(top_b, "row", 1)
+    u1, x1, w = call(
         second_kernel,
-        [shape(NB, NB), shape(NB, HALF), shape(HALF, HALF), shape(HALF, HALF)],
-        5 * 10**9,
-        pos, x0, lead[0], lead[1], other, other_next,
+        [shape(NB, NB)] * 3,
+        10**10,
+        pos, x0, lead[0], lead[1], lead_other, lead_next,
         smem=1,
     )
-    left, rest = after((left, rest))
-    right += [swap(left[a], "col", 1) for a in range(1, loc_rows)]
-    u1, x1, w = call(
-        third_kernel, [shape(NB, NB)] * 3, 5 * 10**9, x0, u01, u_half, x_half, rest
-    )
-    top_a, top_b, right, x1 = after((top_a, top_b, right, x1))
-    other_a, other_b = swap(top_a, "row", 1), swap(top_b, "row", 1)
-    prows = call(
-        functools.partial(rows_kernel, loc_rows),
-        [shape(NB, NB)] * (2 * loc_rows),
-        2 * 10**9,
-        pos, x0, x1, w, *left, *right,
-        smem=1,
-    )
+    right, other_a, other_b, x1 = after((right, other_a, other_b, x1))
     out = call(
         functools.partial(last_kernel, loc_rows, loc_cols),
         shape(*own.shape),
-        3 * 10**9,
-        pos, own, top_a, top_b, other_a, other_b, u0, x0, u1, x1, w, *prows,
+        10**7,
+        pos, own, top_a, top_b, other_a, other_b, u0, x0, u1, x1, w, *left, *right,
         smem=1,
         vmem=24,
+        scratch=[pltpu.VMEM((2 * loc_rows, NB, NB), jnp.float32)],
     )
     return out.reshape(trailing_in.shape)
 

time: 74.9 us -> 72.4 us (0.967)
  waiting for transfers between devices: 24.7 us -> 22.2 us
  Pallas kernels: 26.3 us -> 25 us
  starting transfers between devices: 21.3 us -> 22.6 us
    ppermute x21, waiting for transfers between devices: 24.7 us -> 22.2 us  [swap(): return lax.ppermute(value, axis, [(i, i ^ bits) for i in range(size)])]
    pallas_call x6 -> x4, Pallas kernels: 26.3 us -> 25 us  [call(): pl.pallas_call(kernel, out_shape=out_shape, in_specs=[SMEM] * smem + [VME...]
    ppermute x21, starting transfers between devices: 21.3 us -> 22.6 us  [swap(): return lax.ppermute(value, axis, [(i, i ^ bits) for i in range(size)])]
  transfers between devices with their start and end apart: 21 -> 21, of which waited for: 14 -> 9; matrix products, arithmetic and copies ran while one was open for 1% -> 1% of each run, Pallas kernels for 28% -> 26%
where the time goes in v1:
time: 72.4 us; the launch traced here: 72.2 us
  Pallas kernels  25 us (35%)
  starting transfers between devices  22.6 us (31%)
  waiting for transfers between devices  22.2 us (31%)
  local copies, waits for them, and re-layouts  1.65 us (2%)
    pallas_call x4, Pallas kernels, call(): pl.pallas_call(kernel, out_shape=out_shape, in_specs=[SMEM] * smem + [VME...  25 us
    ppermute x21, starting transfers between devices, swap(): return lax.ppermute(value, axis, [(i, i ^ bits) for i in range(size)])  22.6 us
    ppermute x21, waiting for transfers between devices, swap(): return lax.ppermute(value, axis, [(i, i ^ bits) for i in range(size)])  22.2 us
    unnamed x4, local copies, waits for them, and re-layouts  1.6 us
  transfers between devices with their start and end apart: 21, of which 9 were waited for; matrix products, arithmetic and copies ran while one was open for 1% of the time, Pallas kernels for 26%

profile of v1, /device:TPU:0, one launch (start us, length us, event | category | flops | bytes accessed | tf_op | source)
XLA Modules:
  0.0 72.2 jit_solution(10939965501468786410)
XLA Ops:
  0.0 1.6 %copy-done = f32[2,1,256,4,1,256]{5,4,3,2,1,0:T(1,128)S(1)} copy-done((f32[2,1,256,4,1,256]{5,4,3,2,1,0:T(1,128)S(1)}, f32[2,1,256,4,1,256]{5,4,3,2,1,0:T(1,128)}, u32[]{:S(2)}) %copy-start) | copy-done | bytes 2097176
  1.6 0.2 shard_map.17
  1.8 3.0 %collective-permute-start.2 = (f32[64,256]{1,0:T(8,128)S(1)}, f32[64,256]{1,0:T(8,128)S(1)}, u32[]{:S(2)}, u32[]{:S(2)}) collective-permute-start(f32[64,256]{1,0:T(8,128)S(1)} %get-tuple-element.82), channel_id=1, source_target_pairs={{0,8},{4,12},{8,0},{12,4},{16,24},{20,28},{24,16},{28,20},{1,9},{5... | collective-permute-start | bytes 196616 | tf_op jit(solution)/shard_map/ppermute | solution.py:275
  4.8 1.5 %collective-permute-start.1 = (f32[64,256]{1,0:T(8,128)S(1)}, f32[64,256]{1,0:T(8,128)S(1)}, u32[]{:S(2)}, u32[]{:S(2)}) collective-permute-start(f32[64,256]{1,0:T(8,128)S(1)} %get-tuple-element.83), channel_id=1, source_target_pairs={{0,16},{4,20},{8,24},{12,28},{16,0},{20,4},{24,8},{28,12},{1,17},{... | collective-permute-start | bytes 196616 | tf_op jit(solution)/shard_map/ppermute | solution.py:275
  6.3 0.8 %collective-permute-done.2 = f32[64,256]{1,0:T(8,128)S(1)} collective-permute-done((f32[64,256]{1,0:T(8,128)S(1)}, f32[64,256]{1,0:T(8,128)S(1)}, u32[]{:S(2)}, u32[]{:S(2)}) %collective-permute-start.2) | collective-permute-done | bytes 65568 | tf_op jit(solution)/shard_map/ppermute | solution.py:275
  7.1 1.9 %collective-permute-done.1 = f32[64,256]{1,0:T(8,128)S(1)} collective-permute-done((f32[64,256]{1,0:T(8,128)S(1)}, f32[64,256]{1,0:T(8,128)S(1)}, u32[]{:S(2)}, u32[]{:S(2)}) %collective-permute-start.1) | collective-permute-done | bytes 65568 | tf_op jit(solution)/shard_map/ppermute | solution.py:275
  9.1 2.4 %collective-permute-done = f32[64,256]{1,0:T(8,128)S(1)} collective-permute-done((f32[64,256]{1,0:T(8,128)S(1)}, f32[64,256]{1,0:T(8,128)S(1)}, u32[]{:S(2)}, u32[]{:S(2)}) %collective-permute-start) | collective-permute-done | bytes 65568 | tf_op jit(solution)/shard_map/ppermute | solution.py:275
  11.5 1.6 %collective-permute-start.3 = (f32[64,256]{1,0:T(8,128)S(1)}, f32[64,256]{1,0:T(8,128)S(1)}, u32[]{:S(2)}, u32[]{:S(2)}) collective-permute-start(f32[64,256]{1,0:T(8,128)S(1)} %select_select_fusion.6), channel_id=1, source_target_pairs={{0,1},{1,0},{2,3},{3,2},{4,5},{5,4},{6,7},{7,6},{8,9},{9,8},{10,11... | collective-permute-start | bytes 196616 | tf_op jit(solution)/shard_map/ppermute | solution.py:275
  13.1 2.6 %collective-permute-start.7 = (f32[64,256]{1,0:T(8,128)S(1)}, f32[64,256]{1,0:T(8,128)S(1)}, u32[]{:S(2)}, u32[]{:S(2)}) collective-permute-start(f32[64,256]{1,0:T(8,128)S(1)} %select_select_fusion.6), channel_id=1, source_target_pairs={{0,2},{1,3},{2,0},{3,1},{4,6},{5,7},{6,4},{7,5},{8,10},{9,11},{10,... | collective-permute-start | bytes 196616 | tf_op jit(solution)/shard_map/ppermute | solution.py:275
  15.7 0.2 collective-permute-start.6
  16.0 0.8 %collective-permute-start.4 = (f32[1024,128]{1,0:T(8,128)S(1)}, f32[1024,128]{1,0:T(8,128)S(1)}, u32[]{:S(2)}, u32[]{:S(2)}) collective-permute-start(f32[1024,128]{1,0:T(8,128)S(1)} %get-tuple-element.42), channel_id=1, source_target_pairs={{0,8},{4,12},{8,0},{12,4},{16,24},{20,28},{24,16},{28,20},{1,9},{5... | collective-permute-start | bytes 1572872 | tf_op jit(solution)/shard_map/ppermute | solution.py:275
  16.7 0.5 collective-permute-start.5
  17.3 2.4 %collective-permute-done.7 = f32[64,256]{1,0:T(8,128)S(1)} collective-permute-done((f32[64,256]{1,0:T(8,128)S(1)}, f32[64,256]{1,0:T(8,128)S(1)}, u32[]{:S(2)}, u32[]{:S(2)}) %collective-permute-start.7) | collective-permute-done | bytes 65568 | tf_op jit(solution)/shard_map/ppermute | solution.py:275
  19.7 2.1 %collective-permute-done.6 = f32[64,256]{1,0:T(8,128)S(1)} collective-permute-done((f32[64,256]{1,0:T(8,128)S(1)}, f32[64,256]{1,0:T(8,128)S(1)}, u32[]{:S(2)}, u32[]{:S(2)}) %collective-permute-start.6) | collective-permute-done | bytes 65568 | tf_op jit(solution)/shard_map/ppermute | solution.py:275
  21.8 0.6 collective-permute-start.8
  22.4 1.4 %collective-permute-start.10 = (f32[128,256]{1,0:T(8,128)S(1)}, f32[128,256]{1,0:T(8,128)S(1)}, u32[]{:S(2)}, u32[]{:S(2)}) collective-permute-start(f32[128,256]{1,0:T(8,128)S(1)} %pad_maximum_fusion.2), channel_id=1, source_target_pairs={{0,24},{4,28},{8,16},{12,20},{16,8},{20,12},{24,0},{28,4},{1,25},{... | collective-permute-start | bytes 393224 | tf_op jit(solution)/shard_map/ppermute | solution.py:275
  23.9 1.5 %collective-permute-start.9 = (f32[128,256]{1,0:T(8,128)S(1)}, f32[128,256]{1,0:T(8,128)S(1)}, u32[]{:S(2)}, u32[]{:S(2)}) collective-permute-start(f32[128,256]{1,0:T(8,128)S(1)} %pad_maximum_fusion.2), channel_id=1, source_target_pairs={{0,16},{4,20},{8,24},{12,28},{16,0},{20,4},{24,8},{28,12},{1,17},{... | collective-permute-start | bytes 393224 | tf_op jit(solution)/shard_map/ppermute | solution.py:275
  25.4 0.1 pad_add_fusion.pos
  25.5 5.9 %collective-permute-done.8 = f32[128,256]{1,0:T(8,128)S(1)} collective-permute-done((f32[128,256]{1,0:T(8,128)S(1)}, f32[128,256]{1,0:T(8,128)S(1)}, u32[]{:S(2)}, u32[]{:S(2)}) %collective-permute-start.8) | collective-permute-done | bytes 131104 | tf_op jit(solution)/shard_map/ppermute | solution.py:275
  31.3 2.1 %collective-permute-start.13 = (f32[256,256]{1,0:T(8,128)S(1)}, f32[256,256]{1,0:T(8,128)S(1)}, u32[]{:S(2)}, u32[]{:S(2)}) collective-permute-start(f32[256,256]{1,0:T(8,128)S(1)} %get-tuple-element.60), channel_id=1, source_target_pairs={{0,2},{1,3},{2,0},{3,1},{4,6},{5,7},{6,4},{7,5},{8,10},{9,11},{10,... | collective-permute-start | bytes 786440 | tf_op jit(solution)/shard_map/ppermute | solution.py:275
  33.7 2.1 %collective-permute-start.14 = (f32[256,256]{1,0:T(8,128)S(1)}, f32[256,256]{1,0:T(8,128)S(1)}, u32[]{:S(2)}, u32[]{:S(2)}) collective-permute-start(f32[256,256]{1,0:T(8,128)S(1)} %get-tuple-element.54), channel_id=1, source_target_pairs={{0,2},{1,3},{2,0},{3,1},{4,6},{5,7},{6,4},{7,5},{8,10},{9,11},{10,... | collective-permute-start | bytes 786440 | tf_op jit(solution)/shard_map/ppermute | solution.py:275
  35.8 1.2 %collective-permute-start.12 = (f32[1024,128]{1,0:T(8,128)S(1)}, f32[1024,128]{1,0:T(8,128)S(1)}, u32[]{:S(2)}, u32[]{:S(2)}) collective-permute-start(f32[1024,128]{1,0:T(8,128)S(1)} %broadcast_select_fusion.3), channel_id=1, source_target_pairs={{0,8},{4,12},{8,0},{12,4},{16,24},{20,28},{24,16},{28,20},{1,9},{5... | collective-permute-start | bytes 1572872 | tf_op jit(solution)/shard_map/ppermute | solution.py:275
  37.0 0.7 %collective-permute-start.11 = (f32[1024,128]{1,0:T(8,128)S(1)}, f32[1024,128]{1,0:T(8,128)S(1)}, u32[]{:S(2)}, u32[]{:S(2)}) collective-permute-start(f32[1024,128]{1,0:T(8,128)S(1)} %broadcast_select_fusion.1), channel_id=1, source_target_pairs={{0,16},{4,20},{8,24},{12,28},{16,0},{20,4},{24,8},{28,12},{1,17},{... | collective-permute-start | bytes 1572872 | tf_op jit(solution)/shard_map/ppermute | solution.py:275
  37.8 8.4 %shard_map.18 = (f32[256,256]{1,0:T(8,128)S(1)}, f32[256,256]{1,0:T(8,128)S(1)}) custom-call(s32[4]{0:T(128)S(1)} %pad_add_fusion.pos, f32[256,256]{1,0:T(8,128)S(1)} %get-tuple-element.55.mine.mine0, f32[256,256]{1,0:T(8,128)S(1)} %collective-permute-done.15.other.other0), custom_call_target="tpu_custom_call" | custom-call | flops 10000000000 | bytes 4194304 | tf_op jit(solution)/shard_map/pallas_call | solution.py:249
  46.2 1.1 %collective-permute-done.13 = f32[256,256]{1,0:T(8,128)S(1)} collective-permute-done((f32[256,256]{1,0:T(8,128)S(1)}, f32[256,256]{1,0:T(8,128)S(1)}, u32[]{:S(2)}, u32[]{:S(2)}) %collective-permute-start.13) | collective-permute-done | bytes 262176 | tf_op jit(solution)/shard_map/ppermute | solution.py:275
  47.3 4.6 %collective-permute-done.14 = f32[256,256]{1,0:T(8,128)S(1)} collective-permute-done((f32[256,256]{1,0:T(8,128)S(1)}, f32[256,256]{1,0:T(8,128)S(1)}, u32[]{:S(2)}, u32[]{:S(2)}) %collective-permute-start.14) | collective-permute-done | bytes 262176 | tf_op jit(solution)/shard_map/ppermute | solution.py:275
  52.1 1.3 %collective-permute-start.16 = (f32[256,256]{1,0:T(8,128)S(1)}, f32[256,256]{1,0:T(8,128)S(1)}, u32[]{:S(2)}, u32[]{:S(2)}) collective-permute-start(f32[256,256]{1,0:T(8,128)S(1)} %broadcast_select_fusion.5.rest_0_), channel_id=1, source_target_pairs={{0,1},{1,0},{2,3},{3,2},{4,5},{5,4},{6,7},{7,6},{8,9},{9,8},{10,11... | collective-permute-start | bytes 786440 | tf_op jit(solution)/shard_map/ppermute | solution.py:275
  53.4 0.8 %collective-permute-start.17 = (f32[256,256]{1,0:T(8,128)S(1)}, f32[256,256]{1,0:T(8,128)S(1)}, u32[]{:S(2)}, u32[]{:S(2)}) collective-permute-start(f32[256,256]{1,0:T(8,128)S(1)} %broadcast_select_fusion.4.rest_1_), channel_id=1, source_target_pairs={{0,1},{1,0},{2,3},{3,2},{4,5},{5,4},{6,7},{7,6},{8,9},{9,8},{10,11... | collective-permute-start | bytes 786440 | tf_op jit(solution)/shard_map/ppermute | solution.py:275
  54.2 0.5 collective-permute-start.19
  54.8 0.9 %collective-permute-done.20.other1 = f32[256,256]{1,0:T(8,128)S(1)} collective-permute-done((f32[256,256]{1,0:T(8,128)S(1)}, f32[256,256]{1,0:T(8,128)S(1)}, u32[]{:S(2)}, u32[]{:S(2)}) %collective-permute-start.20) | collective-permute-done | bytes 262176 | tf_op jit(solution)/shard_map/ppermute | solution.py:275
  55.7 10.2 %shard_map.19 = (f32[256,256]{1,0:T(8,128)S(1)}, f32[256,256]{1,0:T(8,128)S(1)}, f32[256,256]{1,0:T(8,128)S(1)}) custom-call(s32[4]{0:T(128)S(1)} %pad_add_fusion.pos, f32[256,256]{1,0:T(8,128)S(1)} %get-tuple-element.62.x0, f32[256,256]{1,0:T(8,128)S(1)} %get-tuple-element.55.mine.mine0, f32[256,256]{1,0:T(8,128)S(1)} %get-tuple-element.63.mine1, ...), custom_call_target="tpu_custom_call" | custom-call | flops 10000000000 | bytes 4194304 | tf_op jit(solution)/shard_map/pallas_call | solution.py:249
  66.0 6.2 %shard_map.20 = f32[4096,128]{1,0:T(8,128)} custom-call(s32[4]{0:T(128)S(1)} %pad_add_fusion.pos, f32[4096,128]{1,0:T(8,128)S(1)} %bitcast.5, f32[1024,128]{1,0:T(8,128)S(1)} %broadcast_select_fusion.2.mine_a, f32[1024,128]{1,0:T(8,128)S(1)} %broadcast_select_fusion.mine_b, f32[1024,128]{1,0:T(8,128)S(1)} %collective-permute-done.18.other_a, ...), custom_call_target="tpu_custom_call" | custom-call | flops 10000000 | bytes 4194304 | tf_op jit(solution)/shard_map/pallas_call | solution.py:249
  (33 shorter events, 0.7 us)
Async XLA Ops:
  0.0 1.6 %copy-start = (f32[2,1,256,4,1,256]{5,4,3,2,1,0:T(1,128)S(1)}, f32[2,1,256,4,1,256]{5,4,3,2,1,0:T(1,128)}, u32[]{:S(2)}) copy-start(f32[2,1,256,4,1,256]{5,4,3,2,1,0:T(1,128)} %param.1) | copy-start | bytes 6291460
  1.8 5.4 %collective-permute-start.2 = (f32[64,256]{1,0:T(8,128)S(1)}, f32[64,256]{1,0:T(8,128)S(1)}, u32[]{:S(2)}, u32[]{:S(2)}) collective-permute-start(f32[64,256]{1,0:T(8,128)S(1)} %get-tuple-element.82), channel_id=1, source_target_pairs={{0,8},{4,12},{8,0},{12,4},{16,24},{20,28},{24,16},{28,20},{1,9},{5... | collective-permute-start | bytes 196616 | tf_op jit(solution)/shard_map/ppermute | solution.py:275
  4.8 4.3 %collective-permute-start.1 = (f32[64,256]{1,0:T(8,128)S(1)}, f32[64,256]{1,0:T(8,128)S(1)}, u32[]{:S(2)}, u32[]{:S(2)}) collective-permute-start(f32[64,256]{1,0:T(8,128)S(1)} %get-tuple-element.83), channel_id=1, source_target_pairs={{0,16},{4,20},{8,24},{12,28},{16,0},{20,4},{24,8},{28,12},{1,17},{... | collective-permute-start | bytes 196616 | tf_op jit(solution)/shard_map/ppermute | solution.py:275
  6.3 5.2 %collective-permute-start = (f32[64,256]{1,0:T(8,128)S(1)}, f32[64,256]{1,0:T(8,128)S(1)}, u32[]{:S(2)}, u32[]{:S(2)}) collective-permute-start(f32[64,256]{1,0:T(8,128)S(1)} %get-tuple-element.84), channel_id=1, source_target_pairs={{0,24},{4,28},{8,16},{12,20},{16,8},{20,12},{24,0},{28,4},{1,25},{... | collective-permute-start | bytes 196616 | tf_op jit(solution)/shard_map/ppermute | solution.py:275
  11.5 4.5 %collective-permute-start.3 = (f32[64,256]{1,0:T(8,128)S(1)}, f32[64,256]{1,0:T(8,128)S(1)}, u32[]{:S(2)}, u32[]{:S(2)}) collective-permute-start(f32[64,256]{1,0:T(8,128)S(1)} %select_select_fusion.6), channel_id=1, source_target_pairs={{0,1},{1,0},{2,3},{3,2},{4,5},{5,4},{6,7},{7,6},{8,9},{9,8},{10,11... | collective-permute-start | bytes 196616 | tf_op jit(solution)/shard_map/ppermute | solution.py:275
  13.1 6.6 %collective-permute-start.7 = (f32[64,256]{1,0:T(8,128)S(1)}, f32[64,256]{1,0:T(8,128)S(1)}, u32[]{:S(2)}, u32[]{:S(2)}) collective-permute-start(f32[64,256]{1,0:T(8,128)S(1)} %select_select_fusion.6), channel_id=1, source_target_pairs={{0,2},{1,3},{2,0},{3,1},{4,6},{5,7},{6,4},{7,5},{8,10},{9,11},{10,... | collective-permute-start | bytes 196616 | tf_op jit(solution)/shard_map/ppermute | solution.py:275
  15.7 6.1 %collective-permute-start.6 = (f32[64,256]{1,0:T(8,128)S(1)}, f32[64,256]{1,0:T(8,128)S(1)}, u32[]{:S(2)}, u32[]{:S(2)}) collective-permute-start(f32[64,256]{1,0:T(8,128)S(1)} %select_select_fusion.6), channel_id=1, source_target_pairs={{0,3},{1,2},{2,1},{3,0},{4,7},{5,6},{6,5},{7,4},{8,11},{9,10},{10,... | collective-permute-start | bytes 196616 | tf_op jit(solution)/shard_map/ppermute | solution.py:275
  16.0 17.5 %collective-permute-start.4 = (f32[1024,128]{1,0:T(8,128)S(1)}, f32[1024,128]{1,0:T(8,128)S(1)}, u32[]{:S(2)}, u32[]{:S(2)}) collective-permute-start(f32[1024,128]{1,0:T(8,128)S(1)} %get-tuple-element.42), channel_id=1, source_target_pairs={{0,8},{4,12},{8,0},{12,4},{16,24},{20,28},{24,16},{28,20},{1,9},{5... | collective-permute-start | bytes 1572872 | tf_op jit(solution)/shard_map/ppermute | solution.py:275
  16.7 16.7 %collective-permute-start.5 = (f32[1024,128]{1,0:T(8,128)S(1)}, f32[1024,128]{1,0:T(8,128)S(1)}, u32[]{:S(2)}, u32[]{:S(2)}) collective-permute-start(f32[1024,128]{1,0:T(8,128)S(1)} %get-tuple-element.43), channel_id=1, source_target_pairs={{0,16},{4,20},{8,24},{12,28},{16,0},{20,4},{24,8},{28,12},{1,17},{... | collective-permute-start | bytes 1572872 | tf_op jit(solution)/shard_map/ppermute | solution.py:275
  21.8 9.5 %collective-permute-start.8 = (f32[128,256]{1,0:T(8,128)S(1)}, f32[128,256]{1,0:T(8,128)S(1)}, u32[]{:S(2)}, u32[]{:S(2)}) collective-permute-start(f32[128,256]{1,0:T(8,128)S(1)} %pad_maximum_fusion.2), channel_id=1, source_target_pairs={{0,8},{4,12},{8,0},{12,4},{16,24},{20,28},{24,16},{28,20},{1,9},{5... | collective-permute-start | bytes 393224 | tf_op jit(solution)/shard_map/ppermute | solution.py:275
  22.4 11.0 %collective-permute-start.10 = (f32[128,256]{1,0:T(8,128)S(1)}, f32[128,256]{1,0:T(8,128)S(1)}, u32[]{:S(2)}, u32[]{:S(2)}) collective-permute-start(f32[128,256]{1,0:T(8,128)S(1)} %pad_maximum_fusion.2), channel_id=1, source_target_pairs={{0,24},{4,28},{8,16},{12,20},{16,8},{20,12},{24,0},{28,4},{1,25},{... | collective-permute-start | bytes 393224 | tf_op jit(solution)/shard_map/ppermute | solution.py:275
  23.9 9.6 %collective-permute-start.9 = (f32[128,256]{1,0:T(8,128)S(1)}, f32[128,256]{1,0:T(8,128)S(1)}, u32[]{:S(2)}, u32[]{:S(2)}) collective-permute-start(f32[128,256]{1,0:T(8,128)S(1)} %pad_maximum_fusion.2), channel_id=1, source_target_pairs={{0,16},{4,20},{8,24},{12,28},{16,0},{20,4},{24,8},{28,12},{1,17},{... | collective-permute-start | bytes 393224 | tf_op jit(solution)/shard_map/ppermute | solution.py:275
  31.3 16.0 %collective-permute-start.13 = (f32[256,256]{1,0:T(8,128)S(1)}, f32[256,256]{1,0:T(8,128)S(1)}, u32[]{:S(2)}, u32[]{:S(2)}) collective-permute-start(f32[256,256]{1,0:T(8,128)S(1)} %get-tuple-element.60), channel_id=1, source_target_pairs={{0,2},{1,3},{2,0},{3,1},{4,6},{5,7},{6,4},{7,5},{8,10},{9,11},{10,... | collective-permute-start | bytes 786440 | tf_op jit(solution)/shard_map/ppermute | solution.py:275
  33.7 18.2 %collective-permute-start.14 = (f32[256,256]{1,0:T(8,128)S(1)}, f32[256,256]{1,0:T(8,128)S(1)}, u32[]{:S(2)}, u32[]{:S(2)}) collective-permute-start(f32[256,256]{1,0:T(8,128)S(1)} %get-tuple-element.54), channel_id=1, source_target_pairs={{0,2},{1,3},{2,0},{3,1},{4,6},{5,7},{6,4},{7,5},{8,10},{9,11},{10,... | collective-permute-start | bytes 786440 | tf_op jit(solution)/shard_map/ppermute | solution.py:275
  35.8 2.0 %collective-permute-start.15 = (f32[256,256]{1,0:T(8,128)S(1)}, f32[256,256]{1,0:T(8,128)S(1)}, u32[]{:S(2)}, u32[]{:S(2)}) collective-permute-start(f32[256,256]{1,0:T(8,128)S(1)} %get-tuple-element.77), channel_id=1, source_target_pairs={{0,4},{4,0},{8,12},{12,8},{16,20},{20,16},{24,28},{28,24},{1,5},{5... | collective-permute-start | bytes 786440 | tf_op jit(solution)/shard_map/ppermute | solution.py:275
  35.8 16.1 %collective-permute-start.12 = (f32[1024,128]{1,0:T(8,128)S(1)}, f32[1024,128]{1,0:T(8,128)S(1)}, u32[]{:S(2)}, u32[]{:S(2)}) collective-permute-start(f32[1024,128]{1,0:T(8,128)S(1)} %broadcast_select_fusion.3), channel_id=1, source_target_pairs={{0,8},{4,12},{8,0},{12,4},{16,24},{20,28},{24,16},{28,20},{1,9},{5... | collective-permute-start | bytes 1572872 | tf_op jit(solution)/shard_map/ppermute | solution.py:275
  37.0 14.9 %collective-permute-start.11 = (f32[1024,128]{1,0:T(8,128)S(1)}, f32[1024,128]{1,0:T(8,128)S(1)}, u32[]{:S(2)}, u32[]{:S(2)}) collective-permute-start(f32[1024,128]{1,0:T(8,128)S(1)} %broadcast_select_fusion.1), channel_id=1, source_target_pairs={{0,16},{4,20},{8,24},{12,28},{16,0},{20,4},{24,8},{28,12},{1,17},{... | collective-permute-start | bytes 1572872 | tf_op jit(solution)/shard_map/ppermute | solution.py:275
  52.1 13.9 %collective-permute-start.16 = (f32[256,256]{1,0:T(8,128)S(1)}, f32[256,256]{1,0:T(8,128)S(1)}, u32[]{:S(2)}, u32[]{:S(2)}) collective-permute-start(f32[256,256]{1,0:T(8,128)S(1)} %broadcast_select_fusion.5.rest_0_), channel_id=1, source_target_pairs={{0,1},{1,0},{2,3},{3,2},{4,5},{5,4},{6,7},{7,6},{8,9},{9,8},{10,11... | collective-permute-start | bytes 786440 | tf_op jit(solution)/shard_map/ppermute | solution.py:275
  53.4 12.5 %collective-permute-start.17 = (f32[256,256]{1,0:T(8,128)S(1)}, f32[256,256]{1,0:T(8,128)S(1)}, u32[]{:S(2)}, u32[]{:S(2)}) collective-permute-start(f32[256,256]{1,0:T(8,128)S(1)} %broadcast_select_fusion.4.rest_1_), channel_id=1, source_target_pairs={{0,1},{1,0},{2,3},{3,2},{4,5},{5,4},{6,7},{7,6},{8,9},{9,8},{10,11... | collective-permute-start | bytes 786440 | tf_op jit(solution)/shard_map/ppermute | solution.py:275
  54.1 1.5 %collective-permute-start.20 = (f32[256,256]{1,0:T(8,128)S(1)}, f32[256,256]{1,0:T(8,128)S(1)}, u32[]{:S(2)}, u32[]{:S(2)}) collective-permute-start(f32[256,256]{1,0:T(8,128)S(1)} %get-tuple-element.63.mine1), channel_id=1, source_target_pairs={{0,4},{4,0},{8,12},{12,8},{16,20},{20,16},{24,28},{28,24},{1,5},{5... | collective-permute-start | bytes 786440 | tf_op jit(solution)/shard_map/ppermute | solution.py:275
  54.2 11.8 %collective-permute-start.19 = (f32[1024,128]{1,0:T(8,128)S(1)}, f32[1024,128]{1,0:T(8,128)S(1)}, u32[]{:S(2)}, u32[]{:S(2)}) collective-permute-start(f32[1024,128]{1,0:T(8,128)S(1)} %broadcast_select_fusion.mine_b), channel_id=1, source_target_pairs={{0,4},{4,0},{8,12},{12,8},{16,20},{20,16},{24,28},{28,24},{1,5},{5... | collective-permute-start | bytes 1572872 | tf_op jit(solution)/shard_map/ppermute | solution.py:275
  54.7 11.3 %copy-start.1 = (f32[2,1,256,4,1,256]{5,4,3,2,1,0:T(1,128)S(1)}, f32[2,1,256,4,1,256]{5,4,3,2,1,0:T(1,128)}, u32[]{:S(2)}) copy-start(f32[2,1,256,4,1,256]{5,4,3,2,1,0:T(1,128)} %param.1) | copy-start | bytes 6291460
  54.7 11.2 %collective-permute-start.18 = (f32[1024,128]{1,0:T(8,128)S(1)}, f32[1024,128]{1,0:T(8,128)S(1)}, u32[]{:S(2)}, u32[]{:S(2)}) collective-permute-start(f32[1024,128]{1,0:T(8,128)S(1)} %broadcast_select_fusion.2.mine_a), channel_id=1, source_target_pairs={{0,4},{4,0},{8,12},{12,8},{16,20},{20,16},{24,28},{28,24},{1,5},{5... | collective-permute-start | bytes 1572872 | tf_op jit(solution)/shard_map/ppermute | solution.py:275
